TPU v7x, 256 devices: a whole 4x4x8 slice. The times are simulated.
256 devices in a mesh: kv: 32 (over x, z), head: 8 (over y, core).
Axes of the slice: x: 4, y: 4, z: 8, core: 2. Of those that a mesh axis runs over, the one named last changes fastest.
Arguments:
- queries: bfloat16 [256, 16384], P(None, 'head'), may hold values from -16 to 16
- cache_keys: bfloat16 [81920, 1024], P('kv', 'head'), may hold values from -5 to 5
- cache_values: bfloat16 [81920, 1024], P('kv', 'head'), may hold values from -6 to 6
- residual: bfloat16 [256, 16384], P('kv', 'head'), may hold values from -12 to 12
- norm_gain: float32 [16384], P('head'), may hold values from 0.1 to 1.9
- w_gate: bfloat16 [16384, 28672], P('head', 'kv'), may hold values from -0.046875 to 0.046875
- w_up: bfloat16 [16384, 28672], P('head', 'kv'), may hold values from -0.046875 to 0.046875
- w_down: bfloat16 [28672, 16384], P('kv', 'head'), may hold values from -0.03125 to 0.03125
Outputs:
- attended: bfloat16 [256, 16384], P('kv', 'head')
- layer_out: bfloat16 [256, 16384], P('kv', 'head')
All inputs are finite; a program needn't handle non-finite values.
Results may differ from a plain program's by a relative error of at most 0.008.
Values may be sent and summed in bfloat16 or wider, within the bound.
A program may use at most 128 MiB of HBM per device.

v0:
```python
import jax
import jax.numpy as jnp
from jax import lax
from jax.sharding import PartitionSpec as P

HD = 128
D = 16384


EPSILON = 1e-05


def local_attention(queries, cache_keys, cache_values):
    row_count = queries.shape[0]
    kv_local = cache_keys.shape[1] // HD
    group_size = queries.shape[1] // (kv_local * HD)
    score_scale = HD ** (-0.5)
    query_block = queries
    query_block = query_block.reshape(row_count * group_size, HD)
    scores = (
        lax.dot_general(
            query_block, cache_keys, (((1,), (1,)), ((), ())), preferred_element_type=jnp.float32
        )
        * score_scale
    )
    peak = jnp.max(scores, axis=1)
    expd = jnp.exp(scores - peak[:, None])
    total = jnp.sum(expd, axis=1)
    partial_out = jnp.dot(
        expd.astype(jnp.bfloat16), cache_values, preferred_element_type=jnp.float32
    )
    outputs = partial_out.reshape(row_count, group_size * HD)
    maxima = peak.reshape(row_count, group_size)
    totals = total.reshape(row_count, group_size)
    return (outputs, maxima, totals)


def body(queries, cache_keys, cache_values, residual, norm_gain, w_gate, w_up, w_down):
    row_count = queries.shape[0]
    block_out, block_max, block_den = local_attention(queries, cache_keys, cache_values)
    local_heads = block_max.shape[1]
    row_top = lax.pmax(block_max, "kv")
    factor = jnp.exp(block_max - row_top)
    scaled = (block_out.reshape(row_count, local_heads, HD) * factor[:, :, None]).reshape(
        row_count, local_heads * HD
    )
    numer, denom = (
        lax.psum_scatter(scaled, "kv", scatter_dimension=0, tiled=True),
        lax.psum_scatter(block_den * factor, "kv", scatter_dimension=0, tiled=True),
    )
    own_rows = numer.shape[0]
    attended = (
        (numer.reshape(own_rows, local_heads, HD) / denom[:, :, None])
        .reshape(own_rows, local_heads * HD)
        .astype(jnp.bfloat16)
    )
    stream = residual.astype(jnp.float32) + attended.astype(jnp.float32)
    squares = lax.psum(jnp.sum(stream * stream, axis=1), "head")
    normed = (stream * lax.rsqrt(squares / D + EPSILON)[:, None] * norm_gain[None, :]).astype(
        jnp.bfloat16
    )
    ff_local = w_gate.shape[1]
    piece = lax.all_gather(normed, "kv", axis=0, tiled=True)
    gate_part = jnp.dot(piece, w_gate, preferred_element_type=jnp.float32)
    up_part = jnp.dot(piece, w_up, preferred_element_type=jnp.float32)
    both_parts = jnp.concatenate([gate_part, up_part], axis=1)
    summed = lax.psum(both_parts, "head")
    hidden = (jax.nn.silu(summed[:, :ff_local]) * summed[:, ff_local:]).astype(jnp.bfloat16)
    ffn_out = lax.psum_scatter(
        jnp.dot(hidden, w_down, preferred_element_type=jnp.float32),
        "kv",
        scatter_dimension=0,
        tiled=True,
    )
    layer_out = (stream + ffn_out).astype(jnp.bfloat16)
    return (attended, layer_out)


def solution(mesh):
    in_specs = (
        P(None, "head"),
        P("kv", "head"),
        P("kv", "head"),
        P("kv", "head"),
        P("head"),
        P("head", "kv"),
        P("head", "kv"),
        P("kv", "head"),
    )
    out_specs = (P("kv", "head"), P("kv", "head"))
    return jax.shard_map(body, mesh=mesh, in_specs=in_specs, out_specs=out_specs, check_vma=False)
```

profile of v0, /device:TPU:32, one launch (start us, length us, event | category | flops | bytes accessed | tf_op | source)
XLA Modules:
  0.0 809.0 jit_solution(14774405259362434027)
XLA Ops:
  7.2 0.0 copy-start
  7.2 0.0 reduce-scatter.3.cloned.1.call-start
  7.2 1.6 reshape.24
  8.8 0.0 copy-done
  8.9 16.1 %multiply_reduce_fusion = (f32[4096]{0:T(1024)S(1)}, f32[4096,2560]{0,1:T(8,128)}) fusion(bf16[4096,128]{1,0:T(8,128)(2,1)S(1)} %reshape.24, bf16[2560,128]{1,0:T(8,128)(2,1)S(1)} %copy-done), kind=kOutput, calls=%fused_computation.1 | convolution fusion | flops 2705321984 | bytes 43663360 | tf_op jit(solution)/shard_map/dot_general | solution.py:21
  25.0 0.1 reshape.25
  25.1 0.0 copy-start.2
  25.1 16.8 %fusion = f32[4096]{0:T(1024)S(1)} fusion(f32[4096,2560]{0,1:T(8,128)} %get-tuple-element.7, f32[4096]{0:T(1024)S(1)} %get-tuple-element.6), kind=kLoop, calls=%fused_computation.2 | loop fusion | flops 31453184 | bytes 41975808 | tf_op jit(solution)/shard_map/reduce_sum | solution.py:28
  41.9 0.0 copy-done.2
  41.9 17.9 %fusion.2 = f32[4096,128]{1,0:T(8,128)} fusion(bf16[2560,128]{1,0:T(8,128)(2,1)S(1)} %copy-done.2, f32[4096,2560]{0,1:T(8,128)} %get-tuple-element.7, f32[4096]{0:T(1024)S(1)} %get-tuple-element.6), kind=kOutput, calls=%fused_computation.4 | convolution fusion | flops 2715811840 | bytes 44711936 | tf_op jit(solution)/shard_map/dot_general | solution.py:29
  59.8 1.7 reshape_reshape.3
  61.5 0.1 reshape.26
  61.6 140.3 %pmax.7 = f32[256,16]{1,0:T(8,128)S(1)} all-reduce(f32[256,16]{1,0:T(8,128)S(1)} %reshape.25), channel_id=1, replica_groups=mesh['kv'=32,'head'=8] {'kv'}, use_global_device_ids=true, to_apply=%region_1.0 | all-reduce | flops 4096 | bytes 32768 | tf_op jit(solution)/shard_map/pmax | solution.py:42
  201.9 0.6 mul.48
  202.5 0.0 copy-start.8
  202.5 0.0 copy-start.3
  202.5 0.0 copy-start.5
  202.6 2.4 bitcast_multiply_fusion
  205.0 0.0 reduce-scatter.3.cloned.1.call-update
  205.0 0.0 all-gather.2.cloned.1.call-start
  205.1 0.0 copy-done.8
  205.1 0.6 dynamic-slice
  206.3 140.2 %all-reduce = f32[256,16]{1,0:T(8,128)S(1)} all-reduce(f32[256,16]{1,0:T(8,128)S(1)} %get-tuple-element.4), channel_id=3, replica_groups=mesh['kv'=32,'head'=8] {'kv'}, use_global_device_ids=true, to_apply=%region_4.0.clone | all-reduce | flops 4096 | bytes 32768
  346.5 0.1 copy.12
  346.6 72.6 %reduce-scatter.3.cloned.1.call-done = f32[8,2048]{1,0:T(8,128)} async-done(((f32[256,2048]{1,0:T(8,128)}), f32[8,2048]{1,0:T(8,128)}) %reduce-scatter.3.cloned.1.call-update) | async-done | bytes 65552 | tf_op jit(solution)/shard_map/reduce_scatter | solution.py:48
  419.2 0.0 copy-done.3
  419.2 1.0 multiply_reduce_fusion.1
  420.3 12.4 %psum.14 = f32[8]{0:T(128)S(1)} all-reduce(f32[8]{0:T(128)S(1)} %get-tuple-element.2), channel_id=1, replica_groups=mesh['kv'=32,'head'=8] {'head'}, use_global_device_ids=true, to_apply=%region_6.0 | all-reduce | flops 8 | bytes 64 | tf_op jit(solution)/shard_map/psum | solution.py:58
  432.7 0.0 copy-done.5
  432.7 0.7 multiply_convert_fusion
  433.4 0.0 all-gather.2.cloned.1.call-update
  433.4 0.2 all-reduce.3.cloned.1.call-start
  433.7 72.1 %all-gather.2.cloned.1.call-done = bf16[256,2048]{1,0:T(8,128)(2,1)} async-done(((bf16[8,2048]{1,0:T(8,128)(2,1)}), bf16[256,2048]{1,0:T(8,128)(2,1)}) %all-gather.2.cloned.1.call-update) | async-done | bytes 1048592 | tf_op jit(solution)/shard_map/all_gather | solution.py:63
  505.8 3.8 fusion.14
  509.5 0.0 copy-done.6
  509.6 0.0 copy-done.7
  509.6 1.3 fusion.13
  510.8 1.4 pad_maximum_fusion
  512.2 0.0 all-reduce.3.cloned.1.call-update
  512.2 0.0 copy-start.1
  512.2 0.0 reduce-scatter.5.cloned.1.call-start
  512.3 68.7 %all-reduce.3.cloned.1.call-done = f32[256,1792]{1,0:T(8,128)} async-done(((f32[256,1792]{1,0:T(8,128)}), f32[256,1792]{1,0:T(8,128)}) %all-reduce.3.cloned.1.call-update) | async-done | bytes 1835024 | tf_op jit(solution)/shard_map/psum | solution.py:67
  581.0 5.2 fusion.5
  586.2 0.0 reduce-scatter.5.cloned.1.call-update
  586.3 214.8 %reduce-scatter.5.cloned.1.call-done = f32[8,2048]{1,0:T(8,128)} async-done(((f32[256,2048]{1,0:T(8,128)}), f32[8,2048]{1,0:T(8,128)}) %reduce-scatter.5.cloned.1.call-update) | async-done | bytes 65552 | tf_op jit(solution)/shard_map/reduce_scatter | solution.py:69
  801.0 0.0 copy-done.4
  801.0 1.5 add_convert_fusion
  802.5 0.0 copy-done.1
  (6 shorter events, 0.0 us)
Async XLA Ops:
  7.2 1.7 copy-start
  7.2 412.0 %reduce-scatter.3.cloned.1.call-start = ((), (), s32[]{:S(2)}) async-start(), calls=%async_computation.2 | async-start | bytes 2162688 | tf_op jit(solution)/shard_map/reduce_scatter | solution.py:48
  25.1 16.8 %copy-start.2 = (bf16[2560,128]{1,0:T(8,128)(2,1)S(1)}, bf16[2560,128]{1,0:T(8,128)(2,1)}, u32[]{:S(2)}) copy-start(bf16[2560,128]{1,0:T(8,128)(2,1)} %param.10) | copy-start | bytes 1966084
  202.5 2.5 copy-start.8
  202.5 216.7 %copy-start.3 = (bf16[8,2048]{1,0:T(8,128)(2,1)S(1)}, bf16[8,2048]{1,0:T(8,128)(2,1)}, u32[]{:S(2)}) copy-start(bf16[8,2048]{1,0:T(8,128)(2,1)} %param.11) | copy-start | bytes 98308
  202.5 230.2 %copy-start.5 = (f32[2048]{0:T(1024)S(1)}, f32[2048]{0:T(1024)}, u32[]{:S(2)}) copy-start(f32[2048]{0:T(1024)} %param.12) | copy-start | bytes 24580
  205.0 300.8 %all-gather.2.cloned.1.call-start = ((), (), s32[]{:S(2)}) async-start(), calls=%async_computation.3 | async-start | bytes 1081344 | tf_op jit(solution)/shard_map/all_gather | solution.py:63
  420.3 380.8 %copy-start.4 = (bf16[8,2048]{1,0:T(8,128)(2,1)}, bf16[8,2048]{1,0:T(8,128)(2,1)S(1)}, u32[]{:S(2)}) copy-start(bf16[8,2048]{1,0:T(8,128)(2,1)S(1)} %get-tuple-element.3) | copy-start | bytes 98308
  433.4 147.6 %all-reduce.3.cloned.1.call-start = ((), (), s32[]{:S(2)}) async-start(), calls=%async_computation.4 | async-start | bytes 3670016 | tf_op jit(solution)/shard_map/psum | solution.py:67
  505.8 3.8 copy-start.6
  505.8 3.8 copy-start.7
  512.2 290.3 %copy-start.1 = (bf16[2560,128]{1,0:T(8,128)(2,1)S(1)}, bf16[2560,128]{1,0:T(8,128)(2,1)}, u32[]{:S(2)}) copy-start(bf16[2560,128]{1,0:T(8,128)(2,1)} %param.9) | copy-start | bytes 1966084
  512.2 288.8 %reduce-scatter.5.cloned.1.call-start = ((), (), s32[]{:S(2)}) async-start(), calls=%async_computation.5 | async-start | bytes 2162688 | tf_op jit(solution)/shard_map/reduce_scatter | solution.py:69
Sparse Core Ops, SparseCore 0:
  205.1 214.0 reduce-scatter.2
  433.5 72.1 all-gather.1
  512.3 68.6 all-reduce.2
  586.4 214.5 reduce-scatter.4
where the time goes:
time: 811 us; the launch traced here: 809 us
  waiting for transfers between devices  428 us (53%)
  blocking collectives  293 us (36%)
  matrix products  44.3 us (5%)
  other arithmetic  23.8 us (3%)
  between operations  14.6 us (2%)
    reduce_scatter x1, waiting for transfers between devices, body(): lax.psum_scatter(jnp.dot(hidden, w_down, preferred_element_type=jnp.float...  215 us
    pmax x1, blocking collectives, body(): row_top = lax.pmax(block_max, 'kv')  140 us
    unnamed x1, blocking collectives  140 us
    reduce_scatter x1, waiting for transfers between devices, body(): lax.psum_scatter(scaled, 'kv', scatter_dimension=0, tiled=True)  72.6 us
    all_gather x1, waiting for transfers between devices, body(): piece = lax.all_gather(normed, 'kv', axis=0, tiled=True)  72.1 us
    psum x1, waiting for transfers between devices, body(): summed = lax.psum(both_parts, 'head')  68.7 us
    dot_general x1, matrix products, local_attention(): jnp.dot(expd.astype(jnp.bfloat16), cache_values, preferred_element_type=j...  17.9 us
    reduce_sum x1, other arithmetic, local_attention(): total = jnp.sum(expd, axis=1)  16.8 us
  transfers between devices with their start and end apart: 4, of which 4 were waited for; matrix products, arithmetic and copies ran while one was open for 0% of the time, Pallas kernels for 0%

commit v1 on v0

v1 whole, which is shorter than its diff:
```python
import jax
import jax.numpy as jnp
from jax import lax
from jax.experimental import pallas as pl
from jax.experimental.pallas import tpu as pltpu
from jax.sharding import PartitionSpec as P

MESH = pl.DeviceIdType.MESH
f32, bf16 = jnp.float32, jnp.bfloat16
HD = 128
D = 16384
EPSILON = 1e-05
NX, NZ, NY = 4, 8, 4
NKV = NX * NZ
OWN = 8
CTX = 2560
LOCAL = 2048
UNITS = 896
KC = 512
SCALE = float(HD**-0.5 * 1.4426950408889634)
PIECE = 144
FCH = UNITS // 128
DCH = 4
DCW = LOCAL // DCH
Z_ORDER = (1, 7, 2, 6, 3, 5, 4)


def split2(v):
    hi = v.astype(bf16).astype(f32)
    return hi, v - hi


def split3(v):
    hi, rest = split2(v)
    mid, low = split2(rest)
    return hi, mid, low


def stats_rows(peak, total):
    width = peak.shape[1]
    rows = [*split3(peak), *split2(total), jnp.zeros((11, width), f32)]
    return jnp.concatenate(rows, axis=0).astype(bf16)


def read_stats(ref):
    s = ref[128:PIECE, :].astype(f32)
    return s[0:1] + s[1:2] + s[2:3], s[3:4] + s[4:5]


def wait_bytes(ref, sem):
    pltpu.make_async_copy(ref, ref, sem).wait()


def kernel(
    q, k, v, res, gain, wg, wu, wd, att_out, out,
    vt, qs, sc, sbuf, xbuf, zs, zbuf, stream, ag, xn, ssb, ssr, wgu, wdv,
    gacc, gs, cbuf, ys, yb, hid, dsf, ds, dxb, zs2, dzb,
    w_sem, d_sem, ax_s, ax_r, az_s, az_r, gz_s, gz_r, gx_s, gx_r,
    ss_s, ss_r, c_s, c_r, y_s, y_r, hy_s, hy_r, hc_s, hc_r, dx_s, dx_r, dz_s, dz_r,
):
    kv, hd = lax.axis_index("kv"), lax.axis_index("head")
    x, z = kv // NZ, kv % NZ
    y, c = hd // 2, hd % 2

    def at_x(dx):
        return (((x + dx) % NX) * NZ + z, hd)

    def at_z(o):
        return (x * NZ + (z + o) % NZ, hd)

    def at_y(dy):
        return (kv, ((y + dy) % NY) * 2 + c)

    def at_head(o):
        return (kv, (hd + o) % 8)

    other = (kv, y * 2 + 1 - c)

    def remote(src, dst, send, recv, dev):
        return pltpu.make_async_remote_copy(
            src_ref=src, dst_ref=dst, send_sem=send, recv_sem=recv, device_id=dev, device_id_type=MESH
        )

    for j in range(FCH):
        cols = pl.ds(j * 128, 128)
        pltpu.make_async_copy(wg.at[:, cols], wgu.at[j, :, pl.ds(0, 128)], w_sem).start()
        pltpu.make_async_copy(wu.at[:, cols], wgu.at[j, :, pl.ds(128, 128)], w_sem).start()
    for j in range(DCH):
        pltpu.make_async_copy(wd.at[:, pl.ds(j * DCW, DCW)], wdv.at[j], d_sem).start()

    barrier = pltpu.get_barrier_semaphore()
    peers = [at_x(o) for o in range(1, NX)] + [at_z(o) for o in range(1, NZ)] + [at_head(o) for o in range(1, 8)]
    for dev in peers:
        pl.semaphore_signal(barrier, inc=1, device_id=dev, device_id_type=MESH)

    vt[...] = v[...].astype(f32).T.astype(bf16)

    def arrange(i, _):
        rows = q[pl.ds(pl.multiple_of(i * 16, 16), 16), :].astype(f32)
        for d in range(2):
            tiles = [rows[8 * d : 8 * d + 8, 128 * h : 128 * h + 128] for h in range(16)]
            qs[2 * i + d] = jnp.concatenate(tiles, axis=0).astype(bf16)
        return 0

    lax.fori_loop(0, NKV // 2, arrange, 0)

    def z_to(j):
        d = (j + 1) // 2
        return (z + 4 + d * (1 - 2 * (j % 2))) % NZ

    def pair_of(half):
        return (2, 1) if half == 0 else (3, 0)

    def queries_of(j, half):
        a, b = pair_of(half)
        zt = z_to(j)
        return jnp.concatenate([qs[((x + a) % NX) * NZ + zt], qs[((x + b) % NX) * NZ + zt]], axis=0)

    def scores(i, qb, slot):
        rows = pl.ds(i * KC, KC)
        s = lax.dot_general(k[rows, :], qb, (((1,), (1,)), ((), ())), preferred_element_type=f32)
        sc[slot, rows, :] = s
        return jnp.max(s.reshape(KC // 8, 8, 256), axis=0)

    def add(a, b):
        return b if a is None else a + b

    def both(j, half, top, qb):
        peak = jnp.max(top, axis=0, keepdims=True) * SCALE
        acc = total = following = None
        for i in range(CTX // KC):
            rows = pl.ds(i * KC, KC)
            p = jnp.exp2(sc[half, rows, :] * SCALE - peak)
            total = add(total, jnp.sum(p.reshape(KC // 8, 8, 256), axis=0))
            acc = add(acc, jnp.dot(vt[:, rows], p.astype(bf16), preferred_element_type=f32))
            m = scores(i, qb, 1 - half)
            following = m if following is None else jnp.maximum(following, m)
        total = jnp.sum(total, axis=0, keepdims=True)
        acc = acc.astype(bf16)
        stats = stats_rows(peak, total)
        for n, dx in enumerate(pair_of(half)):
            sbuf[dx, j, :128, :] = acc[:, n * 128 : n * 128 + 128]
            sbuf[dx, j, 128:PIECE, :] = stats[:, n * 128 : n * 128 + 128]
        for dx in pair_of(half):
            if dx:
                remote(sbuf.at[dx, j], xbuf.at[dx - 1, j], ax_s, ax_r.at[dx - 1, j], at_x(dx)).start()
        return following

    def merge(refs):
        stats = [read_stats(r) for r in refs]
        peak = stats[0][0]
        for m, _ in stats[1:]:
            peak = jnp.maximum(peak, m)
        factors = [jnp.exp2(m - peak) for m, _ in stats]
        total = None
        for f, (_, t) in zip(factors, stats):
            total = add(total, f * t)
        return peak, total, factors

    def weighted(refs, weights):
        acc = None
        for r, w in zip(refs, weights):
            acc = add(acc, r[:128, :].astype(f32) * w)
        return acc

    def send_z(g):
        return remote(zs.at[g], zbuf.at[g], az_s, az_r.at[g], (x * NZ + z_to(g), hd))

    def combine(g):
        for dx in range(1, NX):
            remote(sbuf.at[dx, g], xbuf.at[dx - 1, g], ax_s, ax_r.at[dx - 1, g], at_x(dx)).wait_recv()
        refs = [sbuf.at[0, g]] + [xbuf.at[n, g] for n in range(NX - 1)]
        peak, total, factors = merge(refs)
        zs[g, :128, :] = weighted(refs, factors).astype(bf16)
        zs[g, 128:PIECE, :] = stats_rows(peak, total)

    first = queries_of(0, 0)
    top = None
    for i in range(CTX // KC):
        m = scores(i, first, 0)
        top = m if top is None else jnp.maximum(top, m)

    pl.semaphore_wait(barrier, len(peers))

    def attend(j, top):
        top = both(j, 0, top, queries_of(j, 1))
        top = both(j, 1, top, queries_of((j + 1) % NZ, 0))

        @pl.when(j >= 2)
        def _():
            combine(j - 2)
            send_z(j - 2).start()

        return top

    lax.fori_loop(0, NZ, attend, top)
    combine(6)
    send_z(6).start()
    combine(7)
    for g in range(NZ - 1):
        send_z(g).wait_recv()
    refs = [zs.at[NZ - 1]] + [zbuf.at[g] for g in range(NZ - 1)]
    peak, total, factors = merge(refs)
    inv = 1.0 / total
    att = weighted(refs, [f * inv for f in factors]).T
    att = jnp.concatenate([att[8 * h : 8 * h + 8, :] for h in range(16)], axis=1).astype(bf16)
    att_out[...] = att

    st = res[...].astype(f32) + att.astype(f32)
    stream[...] = st
    squares = jnp.broadcast_to(jnp.sum(st * st, axis=1, keepdims=True), (OWN, 128))
    t = st * gain[...]
    ag[kv, :128, :] = jnp.concatenate([t[:, 128 * h : 128 * h + 128] for h in range(16)], axis=0).astype(bf16)
    ag[kv, 128:PIECE, :] = jnp.concatenate(split2(squares), axis=0).astype(bf16)

    def gather_z(o):
        return remote(ag.at[kv], ag.at[kv], gz_s, gz_r.at[o - 1], at_z(o))

    def gather_x(src, dx):
        return remote(ag.at[src], ag.at[src], gx_s, gx_r.at[dx - 1], at_x(dx))

    for o in reversed(Z_ORDER):
        gather_z(o).start()
    for dx in (2, 1, 3):
        gather_x(kv, dx).start()
    for o in Z_ORDER:
        src = x * NZ + (z + NZ - o) % NZ
        remote(ag.at[src], ag.at[src], gz_s, gz_r.at[o - 1], at_z(o)).wait_recv()
        for dx in (2, 1, 3):
            gather_x(src, dx).start()
    for dx in range(1, NX):
        wait_bytes(ag.at[pl.ds(((x + NX - dx) % NX) * NZ, NZ)], gx_r.at[dx - 1])

    def rebuild(i, _):
        a = ag[2 * i].astype(f32)
        b = ag[2 * i + 1].astype(f32)
        rows = pl.ds(pl.multiple_of(i * 16, 16), 16)
        for h in range(16):
            tile = jnp.concatenate([a[8 * h : 8 * h + 8], b[8 * h : 8 * h + 8]], axis=0)
            xn[rows, 128 * h : 128 * h + 128] = tile.astype(bf16)
        ssb[rows, :] = jnp.concatenate([a[128:136] + a[136:144], b[128:136] + b[136:144]], axis=0)
        return 0

    lax.fori_loop(0, NKV // 2, rebuild, 0)

    def square_copy(o):
        to = (hd + o) % 8
        block = (to % 2) * NY + to // 2
        return remote(
            ssb.at[pl.ds(pl.multiple_of(block * 32, 32), 32)], ssr.at[o - 1], ss_s, ss_r.at[o - 1], at_head(o)
        )

    for o in range(1, 8):
        square_copy(o).start()

    wait_bytes(wgu, w_sem)
    mine = pl.ds(pl.multiple_of(c * 128, 128), 128)
    theirs = pl.ds(pl.multiple_of((1 - c) * 128, 128), 128)
    block = c * NY + y
    own32 = pl.ds(pl.multiple_of(block * 32, 32), 32)

    def core_copy(j):
        return remote(gs.at[j], cbuf.at[j], c_s, c_r.at[j], other)

    def sum_cores(j):
        core_copy(j).wait_recv()
        s = gacc[j, mine, :] + cbuf[j].astype(f32)
        gacc[j, mine, :] = s
        ys[j] = s.astype(bf16).reshape(NY, 32, 256)
        for dy in (2, 1, 3):
            remote(ys.at[j, (y + dy) % NY], yb.at[dy - 1, j], y_s, y_r.at[dy - 1], at_y(dy)).start()

    def project(j, _):
        gacc[j] = jnp.dot(xn[...], wgu[j], preferred_element_type=f32)
        gs[j] = gacc[j, theirs, :].astype(bf16)
        core_copy(j).start()

        @pl.when(j >= 3)
        def _():
            sum_cores(j - 3)

        return 0

    lax.fori_loop(0, FCH, project, 0)
    for j in range(FCH - 3, FCH):
        sum_cores(j)
    for o in range(1, 8):
        square_copy(o).wait_recv()
    squares = ssb[own32, :]
    for o in range(7):
        squares = squares + ssr[o]
    scale = lax.rsqrt(squares / D + EPSILON)
    for dy in range(1, NY):
        wait_bytes(yb.at[dy - 1], y_r.at[dy - 1])
    for j in range(FCH):
        s = gacc[j, own32, :]
        for n in range(NY - 1):
            s = s + yb[n, j].astype(f32)
        gate = s[:, :128] * scale
        up = s[:, 128:] * scale
        hid[own32, 128 * j : 128 * j + 128] = (gate / (1.0 + jnp.exp(-gate)) * up).astype(bf16)

    def rows_of(yy, cc):
        return hid.at[pl.ds(pl.multiple_of((cc * NY + yy) * 32, 32), 32)]

    for dy in (2, 1, 3):
        remote(rows_of(y, c), rows_of(y, c), hy_s, hy_r.at[dy - 1], at_y(dy)).start()
    remote(rows_of(y, c), rows_of(y, c), hc_s, hc_r, other).start()
    for dy in (1, 3, 2):
        piece = rows_of((y + NY - dy) % NY, c)
        remote(piece, piece, hy_s, hy_r.at[dy - 1], at_y(dy)).wait_recv()
        remote(piece, piece, hc_s, hc_r, other).start()
    wait_bytes(hid.at[theirs], hc_r)

    wait_bytes(wdv, d_sem)

    def down_x(j, dx):
        return remote(ds.at[j, (x + dx) % NX], dxb.at[dx - 1, j], dx_s, dx_r.at[dx - 1, j], at_x(dx))

    def down(j, _):
        acc = jnp.dot(hid[...], wdv[j], preferred_element_type=f32)
        for h in range(DCW // 128):
            dsf[:, h] = acc[:, 128 * h : 128 * h + 128].reshape(NKV, OWN, 128)
        ds[j] = dsf[...].reshape(NX, NZ * 32, 128).astype(bf16)
        for dx in (2, 1, 3):
            down_x(j, dx).start()
        return 0

    lax.fori_loop(0, DCH, down, 0)

    def sum_x(j, _):
        for dx in range(1, NX):
            down_x(j, dx).wait_recv()
        s = ds[j, x].astype(f32)
        for n in range(NX - 1):
            s = s + dxb[n, j].astype(f32)
        zs2[j] = s.astype(bf16).reshape(NZ, 32, 128)
        for o in reversed(Z_ORDER):
            remote(zs2.at[j, (z + o) % NZ], dzb.at[o - 1, j], dz_s, dz_r.at[o - 1], at_z(o)).start()
        return 0

    lax.fori_loop(0, DCH, sum_x, 0)
    for o in range(1, NZ):
        wait_bytes(dzb.at[o - 1], dz_r.at[o - 1])
    for j in range(DCH):
        s = zs2[j, z].astype(f32)
        for n in range(NZ - 1):
            s = s + dzb[n, j].astype(f32)
        s = jnp.concatenate([s[8 * h : 8 * h + 8] for h in range(DCW // 128)], axis=1)
        cols = slice(j * DCW, j * DCW + DCW)
        out[:, cols] = (stream[:, cols] + s).astype(bf16)

    wait_bytes(sbuf.at[pl.ds(1, 3)], ax_s)
    wait_bytes(zs.at[pl.ds(0, 7)], az_s)
    wait_bytes(ag.at[pl.ds(0, 7)], gz_s)
    wait_bytes(ag.at[pl.ds(0, 24)], gx_s)
    wait_bytes(ssr, ss_s)
    wait_bytes(gs, c_s)
    wait_bytes(yb, y_s)
    wait_bytes(hid.at[pl.ds(0, 96)], hy_s)
    wait_bytes(hid.at[pl.ds(0, 128)], hc_s)
    wait_bytes(dxb, dx_s)
    wait_bytes(dzb, dz_s)


def body(queries, cache_keys, cache_values, residual, norm_gain, w_gate, w_up, w_down):
    vmem = pl.BlockSpec(memory_space=pltpu.VMEM)
    hbm = pl.BlockSpec(memory_space=pl.ANY)
    dma = pltpu.SemaphoreType.DMA
    shape = jax.ShapeDtypeStruct((OWN, LOCAL), bf16)
    scratch = [
        pltpu.VMEM((HD, CTX), bf16),
        pltpu.VMEM((NKV, 128, HD), bf16),
        pltpu.VMEM((2, CTX, 256), f32),
        pltpu.VMEM((NX, NZ, PIECE, 128), bf16),
        pltpu.VMEM((NX - 1, NZ, PIECE, 128), bf16),
        pltpu.VMEM((NZ, PIECE, 128), bf16),
        pltpu.VMEM((NZ - 1, PIECE, 128), bf16),
        pltpu.VMEM((OWN, LOCAL), f32),
        pltpu.VMEM((NKV, PIECE, 128), bf16),
        pltpu.VMEM((256, LOCAL), bf16),
        pltpu.VMEM((256, 128), f32),
        pltpu.VMEM((7, 32, 128), f32),
        pltpu.VMEM((FCH, LOCAL, 256), bf16),
        pltpu.VMEM((DCH, UNITS, DCW), bf16),
        pltpu.VMEM((FCH, 256, 256), f32),
        pltpu.VMEM((FCH, 128, 256), bf16),
        pltpu.VMEM((FCH, 128, 256), bf16),
        pltpu.VMEM((FCH, NY, 32, 256), bf16),
        pltpu.VMEM((NY - 1, FCH, 32, 256), bf16),
        pltpu.VMEM((256, UNITS), bf16),
        pltpu.VMEM((NKV, DCW // 128, OWN, 128), f32),
        pltpu.VMEM((DCH, NX, NZ * 32, 128), bf16),
        pltpu.VMEM((NX - 1, DCH, NZ * 32, 128), bf16),
        pltpu.VMEM((DCH, NZ, 32, 128), bf16),
        pltpu.VMEM((NZ - 1, DCH, 32, 128), bf16),
        dma, dma,
        dma, dma((NX - 1, NZ)),
        dma, dma((NZ - 1,)),
        dma, dma((NZ - 1,)),
        dma, dma((NX - 1,)),
        dma, dma((7,)),
        dma, dma((FCH,)),
        dma, dma((NY - 1,)),
        dma, dma((NY - 1,)),
        dma, dma,
        dma, dma((NX - 1, DCH)),
        dma, dma((NZ - 1,)),
    ]
    return pl.pallas_call(
        kernel,
        out_shape=(shape, shape),
        in_specs=[vmem] * 5 + [hbm] * 3,
        out_specs=(vmem, vmem),
        scratch_shapes=scratch,
        name="layer",
        compiler_params=pltpu.CompilerParams(
            collective_id=0, has_side_effects=True, vmem_limit_bytes=56 * 2**20
        ),
    )(
        queries, cache_keys, cache_values, residual, norm_gain.reshape(1, LOCAL), w_gate, w_up, w_down
    )


def solution(mesh):
    in_specs = (
        P(None, "head"),
        P("kv", "head"),
        P("kv", "head"),
        P("kv", "head"),
        P("head"),
        P("head", "kv"),
        P("head", "kv"),
        P("kv", "head"),
    )
    out_specs = (P("kv", "head"), P("kv", "head"))
    return jax.shard_map(body, mesh=mesh, in_specs=in_specs, out_specs=out_specs, check_vma=False)
```

time: 811 us -> 85.7 us (0.11)
  the two profiles are of different devices: /device:TPU:32 before, /device:TPU:1 now
where the time goes in v1:
time: 85.7 us; the launch traced here: 85.4 us
  Pallas kernels  82 us (96%)
  local copies, waits for them, and re-layouts  2.75 us (3%)
    pallas_call x1, Pallas kernels, body(): pl.pallas_call(kernel, out_shape=(shape, shape), in_specs=[vmem] * 5 + [h...  82 us
    unnamed x2, local copies, waits for them, and re-layouts  2.75 us

profile of v1, /device:TPU:1, one launch (start us, length us, event | category | flops | bytes accessed | tf_op | source)
XLA Modules:
  0.0 85.4 jit_solution(12991518887921576357)
XLA Ops:
  0.6 82.0 %layer.1 = (bf16[8,2048]{1,0:T(8,128)(2,1)}, bf16[8,2048]{1,0:T(8,128)(2,1)}) custom-call(bf16[256,2048]{1,0:T(8,128)(2,1)} %q.1, bf16[2560,128]{1,0:T(8,128)(2,1)} %k.1, bf16[2560,128]{1,0:T(8,128)(2,1)} %v.1, bf16[8,2048]{1,0:T(8,128)(2,1)} %res.1, f32[1,2048]{1,0:T(1,128)} %bitcast.1, bf16[2048,896]{1,0:T(8,128)(2,1)} %wg.1, bf16[2048,896]{1,0:T(8,128)(2,1)} %wu.1, ...), custom_call_target="tpu_custom_call" | custom-call | tf_op jit(solution)/shard_map/layer/pallas_call | solution.py:410
  82.7 1.4 %copy.12 = bf16[8,2048]{1,0:T(8,128)(2,1)} copy(bf16[8,2048]{1,0:T(8,128)(2,1)} %get-tuple-element.4) | data formatting | bytes 65536
  84.1 1.4 %copy.13 = bf16[8,2048]{1,0:T(8,128)(2,1)} copy(bf16[8,2048]{1,0:T(8,128)(2,1)} %get-tuple-element.5) | data formatting | bytes 65536

commit v2 on v1

v2 whole, which is shorter than its diff:
```python
import jax
import jax.numpy as jnp
from jax import lax
from jax.experimental import pallas as pl
from jax.experimental.pallas import tpu as pltpu
from jax.sharding import PartitionSpec as P

MESH = pl.DeviceIdType.MESH
f32, bf16 = jnp.float32, jnp.bfloat16
HD = 128
D = 16384
EPSILON = 1e-05
NX, NZ, NY = 4, 8, 4
NKV = NX * NZ
OWN = 8
CTX = 2560
LOCAL = 2048
UNITS = 896
KC = 256
X_ORDER = (2, 1, 3, 0)
COLS = NX * 128
SCALE = float(HD**-0.5 * 1.4426950408889634)
PIECE = 144
FCH = UNITS // 128
DCH = 4
DCW = LOCAL // DCH
I_ORDER = (0, 3, 1, 2)


def split2(v):
    hi = v.astype(bf16).astype(f32)
    return hi, v - hi


def split3(v):
    hi, rest = split2(v)
    mid, low = split2(rest)
    return hi, mid, low


def stats_rows(peak, total):
    width = peak.shape[1]
    rows = [*split3(peak), *split2(total), jnp.zeros((11, width), f32)]
    return jnp.concatenate(rows, axis=0).astype(bf16)


def read_stats(ref):
    s = ref[128:PIECE, :].astype(f32)
    return s[0:1] + s[1:2] + s[2:3], s[3:4] + s[4:5]


def wait_bytes(ref, sem):
    pltpu.make_async_copy(ref, ref, sem).wait()


def kernel(
    q, k, v, res, gain, wg, wu, wd, att_out, out,
    vt, sc, sbuf, xbuf, zs, zbuf, stream, ag, xn, ssb, ssc, ssr, wgu, wdv,
    gacc, gs, cbuf, ys, yb, hid, dsf, ds, dxb, zs2, dzb,
    w_sem, d_sem, ax_s, ax_r, az_s, az_r, gz_s, gz_r, gx_s, gx_r, gf_r,
    sc_s, sc_r, ss_s, ss_r, c_s, c_r, y_s, y_r, hy_s, hy_r, hc_s, hc_r, dx_s, dx_r, dz_s, dz_r,
):
    kv, hd = lax.axis_index("kv"), lax.axis_index("head")
    x, z = kv // NZ, kv % NZ
    y, c = hd // 2, hd % 2

    def at_x(dx):
        return (((x + dx) % NX) * NZ + z, hd)

    def at_z(o):
        return (x * NZ + (z + o) % NZ, hd)

    def at_y(dy):
        return (kv, ((y + dy) % NY) * 2 + c)

    other = (kv, y * 2 + 1 - c)

    def remote(src, dst, send, recv, dev):
        return pltpu.make_async_remote_copy(
            src_ref=src, dst_ref=dst, send_sem=send, recv_sem=recv, device_id=dev, device_id_type=MESH
        )

    for j in range(FCH):
        cols = pl.ds(j * 128, 128)
        pltpu.make_async_copy(wg.at[:, cols], wgu.at[j, :, pl.ds(0, 128)], w_sem).start()
        pltpu.make_async_copy(wu.at[:, cols], wgu.at[j, :, pl.ds(128, 128)], w_sem).start()
    for j in range(DCH):
        pltpu.make_async_copy(wd.at[:, pl.ds(j * DCW, DCW)], wdv.at[j], d_sem).start()

    barrier = pltpu.get_barrier_semaphore()
    peers = [at_x(o) for o in range(1, NX)] + [at_z(o) for o in range(1, NZ)] + [at_y(o) for o in range(1, NY)] + [other]
    for dev in peers:
        pl.semaphore_signal(barrier, inc=1, device_id=dev, device_id_type=MESH)

    vt[:HD] = v[...].astype(f32).T.astype(bf16)
    vt[HD:] = jnp.ones((16, CTX), bf16)

    def z_off(j):
        i = j % 4
        same = jnp.where(i == 0, 4, jnp.where(i == 1, 2, jnp.where(i == 2, 6, 0)))
        cross = jnp.where(i == 0, 3, jnp.where(i == 1, 5, jnp.where(i == 2, 1, 7)))
        return jnp.where((z + j // 4) % 2 == 0, same, cross)

    def z_to(j):
        return (z + z_off(j)) % NZ

    def queries_of(j):
        zt = z_to(j)
        tiles = []
        for dx in X_ORDER:
            owner = ((x + dx) % NX) * NZ + zt
            rows = q[pl.ds(pl.multiple_of(owner // 2 * 16, 16), 16), :].astype(f32)
            rows = jnp.where(zt % 2 == 0, rows[:8], rows[8:])
            tiles += [rows[:, 128 * h : 128 * h + 128] for h in range(16)]
        return jnp.concatenate(tiles, axis=0).astype(bf16)

    def scores(i, qb, top):
        rows = pl.ds(i * KC, KC)
        s = lax.dot_general(k[rows, :], qb, (((1,), (1,)), ((), ())), preferred_element_type=f32)
        sc[rows, :] = s
        m = jnp.max(s.reshape(KC // 8, 8, COLS), axis=0)
        return m if top is None else jnp.maximum(top, m)

    def add(a, b):
        return b if a is None else a + b

    def step(j, top):
        qb = queries_of((j + 1) % NZ)
        peak = jnp.max(top, axis=0, keepdims=True) * SCALE
        acc = following = None
        for i in range(CTX // KC):
            rows = pl.ds(i * KC, KC)
            p = jnp.exp2(sc[rows, :] * SCALE - peak)
            acc = add(acc, jnp.dot(vt[:, rows], p.astype(bf16), preferred_element_type=f32))
            following = scores(i, qb, following)
        stats = stats_rows(peak, acc[HD : HD + 1])
        acc = acc[:HD].astype(bf16)
        for n, dx in enumerate(X_ORDER):
            cols = slice(n * 128, n * 128 + 128)
            sbuf[dx, j, :HD, :] = acc[:, cols]
            sbuf[dx, j, HD:PIECE, :] = stats[:, cols]
        for dx in X_ORDER[:3]:
            remote(sbuf.at[dx, j], xbuf.at[dx - 1, j], ax_s, ax_r.at[dx - 1, j], at_x(dx)).start()
        return following

    def merge(refs):
        stats = [read_stats(r) for r in refs]
        peak = stats[0][0]
        for m, _ in stats[1:]:
            peak = jnp.maximum(peak, m)
        factors = [jnp.exp2(m - peak) for m, _ in stats]
        total = None
        for f, (_, t) in zip(factors, stats):
            total = add(total, f * t)
        return peak, total, factors

    def weighted(refs, weights):
        acc = None
        for r, w in zip(refs, weights):
            acc = add(acc, r[:128, :].astype(f32) * w)
        return acc

    def combine(g):
        for dx in range(1, NX):
            remote(sbuf.at[dx, g], xbuf.at[dx - 1, g], ax_s, ax_r.at[dx - 1, g], at_x(dx)).wait_recv()
        refs = [sbuf.at[0, g]] + [xbuf.at[n, g] for n in range(NX - 1)]
        peak, total, factors = merge(refs)
        zs[g, :128, :] = weighted(refs, factors).astype(bf16)
        zs[g, 128:PIECE, :] = stats_rows(peak, total)
        off = z_off(g)

        @pl.when(off != 0)
        def _():
            remote(zs.at[g], zbuf.at[off - 1], az_s, az_r.at[off - 1], at_z(off)).start()

    first = queries_of(0)
    top = None
    for i in range(CTX // KC):
        top = scores(i, first, top)

    pl.semaphore_wait(barrier, len(peers))

    def attend(j, top):
        top = step(j, top)

        @pl.when(j >= 2)
        def _():
            combine(j - 2)

        return top

    lax.fori_loop(0, NZ, attend, top)

    def gather_z(o):
        return remote(ag.at[kv], ag.at[kv], gz_s, gz_r.at[o - 1], at_z(o))

    def finish_merge(p):
        @pl.when(z % 2 == p)
        def _():
            for o in range(1, NZ):
                remote(zs.at[0], zbuf.at[o - 1], az_s, az_r.at[o - 1], at_z(o)).wait_recv()
            refs = [zs.at[4 * p + 3]] + [zbuf.at[n] for n in range(NZ - 1)]
            _, total, factors = merge(refs)
            inv = 1.0 / total
            att = weighted(refs, [f * inv for f in factors]).T
            att = jnp.concatenate([att[8 * h : 8 * h + 8, :] for h in range(16)], axis=1).astype(bf16)
            att_out[...] = att
            st = res[...].astype(f32) + att.astype(f32)
            stream[...] = st
            squares = jnp.broadcast_to(jnp.sum(st * st, axis=1, keepdims=True), (OWN, 128))
            t = st * gain[...]
            rows = jnp.concatenate([t[:, 128 * h : 128 * h + 128] for h in range(16)], axis=0)
            ag[kv, :128, :] = rows.astype(bf16)
            ag[kv, 128:PIECE, :] = jnp.concatenate(split2(squares), axis=0).astype(bf16)
            for o in (4, 5, 3, 6, 2, 7, 1):
                gather_z(o).start()

    def gather_x(src, dx, recv):
        return remote(ag.at[src], ag.at[src], gx_s, recv, at_x(dx))

    def source(p, i):
        o = 2 * i + (z + p) % 2
        return o, (z + NZ - o) % NZ

    def spread(p, i):
        o, zo = source(p, i)
        src = x * NZ + zo

        @pl.when(o != 0)
        def _():
            remote(ag.at[src], ag.at[src], gz_s, gz_r.at[o - 1], at_z(o)).wait_recv()

        for n, dx in enumerate((1, 3)):
            gather_x(src, dx, gx_r.at[n, o]).start()

    def forward(p, i):
        n, dx = ((0, 1), (1, 3))[i % 2]
        o, zo = source(p, i)
        src = ((x + NX - dx) % NX) * NZ + zo
        gather_x(src, dx, gx_r.at[n, o]).wait_recv()
        gather_x(src, dx, gf_r.at[p, n]).start()

    def gathered(p):
        for i in I_ORDER:
            n, dx = ((1, 3), (0, 1))[i % 2]
            o, zo = source(p, i)
            gather_x(((x + NX - dx) % NX) * NZ + zo, dx, gx_r.at[n, o]).wait_recv()
        for n in range(2):
            wait_bytes(ag.at[pl.ds(0, 2)], gf_r.at[p, n])

    def rebuild(p):
        def pair(i, _):
            first = (i // 2) * NZ + 4 * (i % 2) + p
            a = ag[first].astype(f32)
            b = ag[first + 2].astype(f32)
            rows = pl.ds(pl.multiple_of(i * 16, 16), 16)
            for h in range(16):
                tile = jnp.concatenate([a[8 * h : 8 * h + 8], b[8 * h : 8 * h + 8]], axis=0)
                xn[p, rows, 128 * h : 128 * h + 128] = tile.astype(bf16)
            ssb[p, rows, :] = jnp.concatenate([a[128:136] + a[136:144], b[128:136] + b[136:144]], axis=0)
            return 0

        lax.fori_loop(0, 8, pair, 0)

    mine = pl.ds(pl.multiple_of(c * 64, 64), 64)
    theirs = pl.ds(pl.multiple_of((1 - c) * 64, 64), 64)

    def rows_at(yy, cc):
        return pl.ds(pl.multiple_of((cc * NY + yy) * 16, 16), 16)

    own16 = rows_at(y, c)

    def square_core(p):
        return remote(ssb.at[p, theirs], ssc.at[p], sc_s, sc_r.at[p], other)

    def square_y(p, dy):
        src = ssb.at[p, rows_at((y + dy) % NY, c)]
        return remote(src, ssr.at[p, dy - 1], ss_s, ss_r.at[p, dy - 1], at_y(dy))

    def core_copy(p, j):
        return remote(gs.at[p, j], cbuf.at[p, j], c_s, c_r.at[p, j], other)

    def project(p):
        square_core(p).start()

        def chunk(j, _):
            gacc[p, j] = jnp.dot(xn[p], wgu[j], preferred_element_type=f32)
            gs[p, j] = gacc[p, j, theirs, :].astype(bf16)
            core_copy(p, j).start()
            return 0

        lax.fori_loop(0, FCH, chunk, 0)

    def sum_cores(p):
        square_core(p).wait_recv()
        ssb[p, mine, :] = ssb[p, mine, :] + ssc[p]
        for dy in (2, 1, 3):
            square_y(p, dy).start()

        def chunk(j, _):
            core_copy(p, j).wait_recv()
            s = gacc[p, j, mine, :] + cbuf[p, j].astype(f32)
            gacc[p, j, mine, :] = s
            ys[p, j] = s.astype(bf16).reshape(NY, 16, 256)
            for dy in (2, 1, 3):
                to = (y + dy) % NY
                remote(ys.at[p, j, to], yb.at[p, dy - 1, j], y_s, y_r.at[p, dy - 1], at_y(dy)).start()
            return 0

        lax.fori_loop(0, FCH, chunk, 0)

    def hid_rows(p, yy):
        return hid.at[p, rows_at(yy, c)]

    def hid_y(p, yy, dy):
        return remote(hid_rows(p, yy), hid_rows(p, yy), hy_s, hy_r.at[p, dy - 1], at_y(dy))

    def hid_core(p, yy):
        return remote(hid_rows(p, yy), hid_rows(p, yy), hc_s, hc_r.at[p], other)

    def activate(p):
        for dy in range(1, NY):
            square_y(p, dy).wait_recv()
        squares = ssb[p, own16, :]
        for n in range(NY - 1):
            squares = squares + ssr[p, n]
        scale = lax.rsqrt(squares / D + EPSILON)
        for dy in range(1, NY):
            wait_bytes(yb.at[p, dy - 1], y_r.at[p, dy - 1])
        for j in range(FCH):
            s = gacc[p, j, own16, :]
            for n in range(NY - 1):
                s = s + yb[p, n, j].astype(f32)
            gate = s[:, :128] * scale
            up = s[:, 128:] * scale
            hid[p, own16, 128 * j : 128 * j + 128] = (gate / (1.0 + jnp.exp(-gate)) * up).astype(bf16)
        for dy in (2, 1, 3):
            hid_y(p, y, dy).start()
        hid_core(p, y).start()

    def hid_forward(p):
        for dy in (1, 3, 2):
            yy = (y + NY - dy) % NY
            hid_y(p, yy, dy).wait_recv()
            hid_core(p, yy).start()

    def down_x(p, j, dx):
        src = ds.at[p, j, (x + dx) % NX]
        return remote(src, dxb.at[p, dx - 1, j], dx_s, dx_r.at[p, dx - 1, j], at_x(dx))

    def down(p):
        wait_bytes(hid.at[p, theirs], hc_r.at[p])

        def chunk(j, _):
            acc = jnp.dot(hid[p], wdv[j], preferred_element_type=f32)
            for h in range(DCW // 128):
                dsf[:, h] = acc[:, 128 * h : 128 * h + 128].reshape(NKV // 2, OWN, 128)
            ds[p, j] = dsf[...].reshape(NX, 128, 128).astype(bf16)
            for dx in (2, 1, 3):
                down_x(p, j, dx).start()
            return 0

        lax.fori_loop(0, DCH, chunk, 0)

    def sum_x(p):
        def chunk(j, _):
            for dx in range(1, NX):
                down_x(p, j, dx).wait_recv()
            s = ds[p, j, x].astype(f32)
            for n in range(NX - 1):
                s = s + dxb[p, n, j].astype(f32)
            zs2[p, j] = s.astype(bf16).reshape(4, 32, 128)
            for i in range(4):
                off = (2 * i + p + NZ - z) % NZ

                @pl.when(off != 0)
                def _():
                    remote(
                        zs2.at[p, j, i], dzb.at[off - 1, j], dz_s, dz_r.at[off - 1], at_z(off)
                    ).start()

            return 0

        lax.fori_loop(0, DCH, chunk, 0)

    def finish(p):
        @pl.when(z % 2 == p)
        def _():
            for o in range(1, NZ):
                wait_bytes(dzb.at[o - 1], dz_r.at[o - 1])
            for j in range(DCH):
                s = zs2[p, j, z // 2].astype(f32)
                for n in range(NZ - 1):
                    s = s + dzb[n, j].astype(f32)
                s = jnp.concatenate([s[8 * h : 8 * h + 8] for h in range(DCW // 128)], axis=1)
                cols = slice(j * DCW, j * DCW + DCW)
                out[:, cols] = (stream[:, cols] + s).astype(bf16)

    combine(6)
    finish_merge(0)
    combine(7)
    for i in I_ORDER:
        spread(0, i)
    finish_merge(1)
    for i in I_ORDER:
        forward(0, i)
    for i in I_ORDER:
        spread(1, i)
    gathered(0)
    rebuild(0)
    wait_bytes(wgu, w_sem)
    project(0)
    for i in I_ORDER:
        forward(1, i)
    sum_cores(0)
    gathered(1)
    rebuild(1)
    project(1)
    activate(0)
    sum_cores(1)
    hid_forward(0)
    wait_bytes(wdv, d_sem)
    activate(1)
    down(0)
    hid_forward(1)
    sum_x(0)
    down(1)
    sum_x(1)
    finish(0)
    finish(1)

    wait_bytes(sbuf.at[pl.ds(1, 3)], ax_s)
    wait_bytes(zs.at[pl.ds(0, 7)], az_s)
    wait_bytes(ag.at[pl.ds(0, 7)], gz_s)
    wait_bytes(ag.at[pl.ds(0, 24)], gx_s)
    wait_bytes(ssc, sc_s)
    wait_bytes(ssr, ss_s)
    wait_bytes(gs, c_s)
    wait_bytes(yb, y_s)
    wait_bytes(hid.at[0, pl.ds(0, 96)], hy_s)
    wait_bytes(hid.at[0], hc_s)
    wait_bytes(dxb, dx_s)
    wait_bytes(dzb, dz_s)


def body(queries, cache_keys, cache_values, residual, norm_gain, w_gate, w_up, w_down):
    vmem = pl.BlockSpec(memory_space=pltpu.VMEM)
    hbm = pl.BlockSpec(memory_space=pl.ANY)
    dma = pltpu.SemaphoreType.DMA
    shape = jax.ShapeDtypeStruct((OWN, LOCAL), bf16)
    scratch = [
        pltpu.VMEM((HD + 16, CTX), bf16),
        pltpu.VMEM((CTX, COLS), f32),
        pltpu.VMEM((NX, NZ, PIECE, 128), bf16),
        pltpu.VMEM((NX - 1, NZ, PIECE, 128), bf16),
        pltpu.VMEM((NZ, PIECE, 128), bf16),
        pltpu.VMEM((NZ - 1, PIECE, 128), bf16),
        pltpu.VMEM((OWN, LOCAL), f32),
        pltpu.VMEM((NKV, PIECE, 128), bf16),
        pltpu.VMEM((2, 128, LOCAL), bf16),
        pltpu.VMEM((2, 128, 128), f32),
        pltpu.VMEM((2, 64, 128), f32),
        pltpu.VMEM((2, NY - 1, 16, 128), f32),
        pltpu.VMEM((FCH, LOCAL, 256), bf16),
        pltpu.VMEM((DCH, UNITS, DCW), bf16),
        pltpu.VMEM((2, FCH, 128, 256), f32),
        pltpu.VMEM((2, FCH, 64, 256), bf16),
        pltpu.VMEM((2, FCH, 64, 256), bf16),
        pltpu.VMEM((2, FCH, NY, 16, 256), bf16),
        pltpu.VMEM((2, NY - 1, FCH, 16, 256), bf16),
        pltpu.VMEM((2, 128, UNITS), bf16),
        pltpu.VMEM((NKV // 2, DCW // 128, OWN, 128), f32),
        pltpu.VMEM((2, DCH, NX, 128, 128), bf16),
        pltpu.VMEM((2, NX - 1, DCH, 128, 128), bf16),
        pltpu.VMEM((2, DCH, 4, 32, 128), bf16),
        pltpu.VMEM((NZ - 1, DCH, 32, 128), bf16),
        dma, dma,
        dma, dma((NX - 1, NZ)),
        dma, dma((NZ - 1,)),
        dma, dma((NZ - 1,)),
        dma, dma((2, NZ)), dma((2, 2)),
        dma, dma((2,)),
        dma, dma((2, NY - 1)),
        dma, dma((2, FCH)),
        dma, dma((2, NY - 1)),
        dma, dma((2, NY - 1)),
        dma, dma((2,)),
        dma, dma((2, NX - 1, DCH)),
        dma, dma((NZ - 1,)),
    ]
    return pl.pallas_call(
        kernel,
        out_shape=(shape, shape),
        in_specs=[vmem] * 5 + [hbm] * 3,
        out_specs=(vmem, vmem),
        scratch_shapes=scratch,
        name="layer",
        compiler_params=pltpu.CompilerParams(
            collective_id=0, has_side_effects=True, vmem_limit_bytes=56 * 2**20
        ),
    )(
        queries, cache_keys, cache_values, residual, norm_gain.reshape(1, LOCAL), w_gate, w_up, w_down
    )


def solution(mesh):
    in_specs = (
        P(None, "head"),
        P("kv", "head"),
        P("kv", "head"),
        P("kv", "head"),
        P("head"),
        P("head", "kv"),
        P("head", "kv"),
        P("kv", "head"),
    )
    out_specs = (P("kv", "head"), P("kv", "head"))
    return jax.shard_map(body, mesh=mesh, in_specs=in_specs, out_specs=out_specs, check_vma=False)
```

time: 85.7 us -> 82.2 us (0.959)
  the two profiles are of different devices: /device:TPU:1 before, /device:TPU:32 now
where the time goes in v2:
time: 82.2 us; the launch traced here: 81.9 us
  Pallas kernels  78.5 us (95%)
  local copies, waits for them, and re-layouts  2.75 us (3%)
    pallas_call x1, Pallas kernels, body(): pl.pallas_call(kernel, out_shape=(shape, shape), in_specs=[vmem] * 5 + [h...  78.5 us
    unnamed x2, local copies, waits for them, and re-layouts  2.75 us

profile of v2, /device:TPU:32, one launch (start us, length us, event | category | flops | bytes accessed | tf_op | source)
XLA Modules:
  0.0 81.9 jit_solution(14704969180969139785)
XLA Ops:
  0.6 78.5 %layer.1 = (bf16[8,2048]{1,0:T(8,128)(2,1)}, bf16[8,2048]{1,0:T(8,128)(2,1)}) custom-call(bf16[256,2048]{1,0:T(8,128)(2,1)} %q.1, bf16[2560,128]{1,0:T(8,128)(2,1)} %k.1, bf16[2560,128]{1,0:T(8,128)(2,1)} %v.1, bf16[8,2048]{1,0:T(8,128)(2,1)} %res.1, f32[1,2048]{1,0:T(1,128)} %bitcast.1, bf16[2048,896]{1,0:T(8,128)(2,1)} %wg.1, bf16[2048,896]{1,0:T(8,128)(2,1)} %wu.1, ...), custom_call_target="tpu_custom_call" | custom-call | tf_op jit(solution)/shard_map/layer/pallas_call | solution.py:491
  79.2 1.4 %copy.12 = bf16[8,2048]{1,0:T(8,128)(2,1)} copy(bf16[8,2048]{1,0:T(8,128)(2,1)} %get-tuple-element.4) | data formatting | bytes 65536
  80.6 1.4 %copy.13 = bf16[8,2048]{1,0:T(8,128)(2,1)} copy(bf16[8,2048]{1,0:T(8,128)(2,1)} %get-tuple-element.5) | data formatting | bytes 65536

commit v3 on v2

--- a/solution.py
+++ b/solution.py
@@ -24,6 +24,8 @@
 FCH = UNITS // 128
 DCH = 4
 DCW = LOCAL // DCH
+SPLIT = 96
+FAR = (4, 5, 3, 6, 2, 7, 1)
 I_ORDER = (0, 3, 1, 2)
 
 
@@ -54,11 +56,12 @@
 
 
 def kernel(
-    q, k, v, res, gain, wg, wu, wd, att_out, out,
+    q_in, k_in, v_in, res_in, gain_in, wg, wu, wd, outs,
+    q, k, v, res, gain, q_sem, k_sem, v_sem, res_sem, gain_sem,
     vt, sc, sbuf, xbuf, zs, zbuf, stream, ag, xn, ssb, ssc, ssr, wgu, wdv,
-    gacc, gs, cbuf, ys, yb, hid, dsf, ds, dxb, zs2, dzb,
-    w_sem, d_sem, ax_s, ax_r, az_s, az_r, gz_s, gz_r, gx_s, gx_r, gf_r,
-    sc_s, sc_r, ss_s, ss_r, c_s, c_r, y_s, y_r, hy_s, hy_r, hc_s, hc_r, dx_s, dx_r, dz_s, dz_r,
+    gacc, gs, cbuf, ys, yb, hid, dsf, ds, dxb, zs2, dzb, fzb, fzs, fxb,
+    w_sem, d_sem, ax_s, ax_r, az_s, az_r, gz_s, gz_r, gx_s, gx_r, hx_s, hx_r, hz_s, hz_r,
+    sc_s, sc_r, ss_s, ss_r, c_s, c_r, y_s, y_r, hy_s, hy_r, hc_s, hc_r, dx_s, dx_r, dz_s, dz_r, fz_s, fz_r, fx_s, fx_r,
 ):
     kv, hd = lax.axis_index("kv"), lax.axis_index("head")
     x, z = kv // NZ, kv % NZ
@@ -80,19 +83,15 @@
             src_ref=src, dst_ref=dst, send_sem=send, recv_sem=recv, device_id=dev, device_id_type=MESH
         )
 
-    for j in range(FCH):
-        cols = pl.ds(j * 128, 128)
-        pltpu.make_async_copy(wg.at[:, cols], wgu.at[j, :, pl.ds(0, 128)], w_sem).start()
-        pltpu.make_async_copy(wu.at[:, cols], wgu.at[j, :, pl.ds(128, 128)], w_sem).start()
-    for j in range(DCH):
-        pltpu.make_async_copy(wd.at[:, pl.ds(j * DCW, DCW)], wdv.at[j], d_sem).start()
+    loads = [(k_in, k, k_sem), (q_in, q, q_sem), (v_in, v, v_sem), (res_in, res, res_sem), (gain_in, gain, gain_sem)]
+    for src, dst, sem in loads:
+        pltpu.make_async_copy(src, dst, sem).start()
 
     barrier = pltpu.get_barrier_semaphore()
     peers = [at_x(o) for o in range(1, NX)] + [at_z(o) for o in range(1, NZ)] + [at_y(o) for o in range(1, NY)] + [other]
     for dev in peers:
         pl.semaphore_signal(barrier, inc=1, device_id=dev, device_id_type=MESH)
 
-    vt[:HD] = v[...].astype(f32).T.astype(bf16)
     vt[HD:] = jnp.ones((16, CTX), bf16)
 
     def z_off(j):
@@ -173,26 +172,49 @@
         def _():
             remote(zs.at[g], zbuf.at[off - 1], az_s, az_r.at[off - 1], at_z(off)).start()
 
+    for src, dst, sem in loads[:2]:
+        pltpu.make_async_copy(src, dst, sem).wait()
     first = queries_of(0)
     top = None
     for i in range(CTX // KC):
         top = scores(i, first, top)
+    for src, dst, sem in loads[2:]:
+        pltpu.make_async_copy(src, dst, sem).wait()
+    for j in range(FCH):
+        cols = pl.ds(j * 128, 128)
+        pltpu.make_async_copy(wg.at[:, cols], wgu.at[j, :, pl.ds(0, 128)], w_sem).start()
+        pltpu.make_async_copy(wu.at[:, cols], wgu.at[j, :, pl.ds(128, 128)], w_sem).start()
+    for j in range(DCH):
+        pltpu.make_async_copy(wd.at[:, pl.ds(j * DCW, DCW)], wdv.at[j], d_sem).start()
+
+    vt[:HD] = v[...].astype(f32).T.astype(bf16)
 
     pl.semaphore_wait(barrier, len(peers))
 
-    def attend(j, top):
-        top = step(j, top)
-
-        @pl.when(j >= 2)
-        def _():
-            combine(j - 2)
-
-        return top
-
-    lax.fori_loop(0, NZ, attend, top)
-
     def gather_z(o):
-        return remote(ag.at[kv], ag.at[kv], gz_s, gz_r.at[o - 1], at_z(o))
+        return remote(part(kv), part(kv), gz_s, gz_r.at[o - 1], at_z(o))
+
+    def part(src):
+        return ag.at[src, pl.ds(0, SPLIT)]
+
+    def rest(src):
+        return ag.at[src, pl.ds(SPLIT, PIECE - SPLIT)]
+
+    def rest_x(src, dx):
+        return remote(rest(src), rest(src), hx_s, hx_r.at[dx - 1], at_x(dx))
+
+    def rest_z(src):
+        for o in FAR:
+            remote(rest(src), rest(src), hz_s, hz_r.at[o - 1], at_z(o)).start()
+
+    def pass_rest(p):
+        @pl.when(z % 2 == p)
+        def _():
+            rest_z(kv)
+            for dx in (1, 3, 2):
+                src = ((x + NX - dx) % NX) * NZ + z
+                rest_x(src, dx).wait_recv()
+                rest_z(src)
 
     def finish_merge(p):
         @pl.when(z % 2 == p)
@@ -204,7 +226,7 @@
             inv = 1.0 / total
             att = weighted(refs, [f * inv for f in factors]).T
             att = jnp.concatenate([att[8 * h : 8 * h + 8, :] for h in range(16)], axis=1).astype(bf16)
-            att_out[...] = att
+            outs[0] = att
             st = res[...].astype(f32) + att.astype(f32)
             stream[...] = st
             squares = jnp.broadcast_to(jnp.sum(st * st, axis=1, keepdims=True), (OWN, 128))
@@ -212,11 +234,28 @@
             rows = jnp.concatenate([t[:, 128 * h : 128 * h + 128] for h in range(16)], axis=0)
             ag[kv, :128, :] = rows.astype(bf16)
             ag[kv, 128:PIECE, :] = jnp.concatenate(split2(squares), axis=0).astype(bf16)
-            for o in (4, 5, 3, 6, 2, 7, 1):
+            for o in FAR:
                 gather_z(o).start()
+            for dx in (2, 1, 3):
+                rest_x(kv, dx).start()
+
+    def attend(j, top):
+        top = step(j, top)
+
+        @pl.when(j >= 2)
+        def _():
+            combine(j - 2)
+
+        @pl.when(j == NZ - 1)
+        def _():
+            finish_merge(0)
+
+        return top
+
+    lax.fori_loop(0, NZ, attend, top)
 
     def gather_x(src, dx, recv):
-        return remote(ag.at[src], ag.at[src], gx_s, recv, at_x(dx))
+        return remote(part(src), part(src), gx_s, recv, at_x(dx))
 
     def source(p, i):
         o = 2 * i + (z + p) % 2
@@ -228,25 +267,20 @@
 
         @pl.when(o != 0)
         def _():
-            remote(ag.at[src], ag.at[src], gz_s, gz_r.at[o - 1], at_z(o)).wait_recv()
-
-        for n, dx in enumerate((1, 3)):
-            gather_x(src, dx, gx_r.at[n, o]).start()
-
-    def forward(p, i):
-        n, dx = ((0, 1), (1, 3))[i % 2]
-        o, zo = source(p, i)
-        src = ((x + NX - dx) % NX) * NZ + zo
-        gather_x(src, dx, gx_r.at[n, o]).wait_recv()
-        gather_x(src, dx, gf_r.at[p, n]).start()
+            remote(part(src), part(src), gz_s, gz_r.at[o - 1], at_z(o)).wait_recv()
+
+        for dx in (2, 1, 3):
+            gather_x(src, dx, gx_r.at[dx - 1, o]).start()
 
     def gathered(p):
         for i in I_ORDER:
-            n, dx = ((1, 3), (0, 1))[i % 2]
             o, zo = source(p, i)
-            gather_x(((x + NX - dx) % NX) * NZ + zo, dx, gx_r.at[n, o]).wait_recv()
-        for n in range(2):
-            wait_bytes(ag.at[pl.ds(0, 2)], gf_r.at[p, n])
+            for dx in range(1, NX):
+                gather_x(((x + NX - dx) % NX) * NZ + zo, dx, gx_r.at[dx - 1, o]).wait_recv()
+
+            @pl.when(o != 0)
+            def _():
+                wait_bytes(ag.at[pl.ds(0, NX), pl.ds(SPLIT, PIECE - SPLIT)], hz_r.at[o - 1])
 
     def rebuild(p):
         def pair(i, _):
@@ -351,16 +385,47 @@
     def down(p):
         wait_bytes(hid.at[p, theirs], hc_r.at[p])
 
-        def chunk(j, _):
+        def chunk(j):
             acc = jnp.dot(hid[p], wdv[j], preferred_element_type=f32)
             for h in range(DCW // 128):
                 dsf[:, h] = acc[:, 128 * h : 128 * h + 128].reshape(NKV // 2, OWN, 128)
             ds[p, j] = dsf[...].reshape(NX, 128, 128).astype(bf16)
+
+        chunk(0)
+        for n in range(4):
+            off, i = owner_of(p, n)
+
+            @pl.when(off != 0)
+            def _():
+                src = ds.at[p, 0, :, pl.ds(pl.multiple_of(32 * i, 32), 32)]
+                remote(src, fzb.at[off - 1], fz_s, fz_r.at[off - 1], at_z(off)).start()
+
+        def later(j, _):
+            chunk(j)
             for dx in (2, 1, 3):
                 down_x(p, j, dx).start()
             return 0
 
-        lax.fori_loop(0, DCH, chunk, 0)
+        lax.fori_loop(1, DCH, later, 0)
+
+    def owner_of(p, n):
+        off = z_off(4 * p + n)
+        return off, ((z + off) % NZ) // 2
+
+    def sum_z(p):
+        @pl.when(z % 2 == p)
+        def _():
+            for o in range(1, NZ):
+                remote(fzb.at[o - 1], fzb.at[o - 1], fz_s, fz_r.at[o - 1], at_z(o)).wait_recv()
+            s = ds[p, 0, :, pl.ds(pl.multiple_of(z // 2 * 32, 32), 32), :].astype(f32)
+            for n in range(NZ - 1):
+                s = s + fzb[n].astype(f32)
+            fzs[...] = s.astype(bf16)
+            for dx in (2, 1, 3):
+                last_x(dx).start()
+
+    def last_x(dx):
+        return remote(fzs.at[(x + dx) % NX], fxb.at[dx - 1], fx_s, fx_r.at[dx - 1], at_x(dx))
 
     def sum_x(p):
         def chunk(j, _):
@@ -370,48 +435,52 @@
             for n in range(NX - 1):
                 s = s + dxb[p, n, j].astype(f32)
             zs2[p, j] = s.astype(bf16).reshape(4, 32, 128)
-            for i in range(4):
-                off = (2 * i + p + NZ - z) % NZ
+            for n in range(4):
+                off, i = owner_of(p, n)
 
                 @pl.when(off != 0)
                 def _():
                     remote(
-                        zs2.at[p, j, i], dzb.at[off - 1, j], dz_s, dz_r.at[off - 1], at_z(off)
+                        zs2.at[p, j, i], dzb.at[off - 1, j - 1], dz_s, dz_r.at[off - 1], at_z(off)
                     ).start()
 
             return 0
 
-        lax.fori_loop(0, DCH, chunk, 0)
+        lax.fori_loop(1, DCH, chunk, 0)
 
     def finish(p):
         @pl.when(z % 2 == p)
         def _():
+            for dx in range(1, NX):
+                last_x(dx).wait_recv()
             for o in range(1, NZ):
                 wait_bytes(dzb.at[o - 1], dz_r.at[o - 1])
             for j in range(DCH):
-                s = zs2[p, j, z // 2].astype(f32)
-                for n in range(NZ - 1):
-                    s = s + dzb[n, j].astype(f32)
+                if j == 0:
+                    s = fzs[x].astype(f32)
+                    for n in range(NX - 1):
+                        s = s + fxb[n].astype(f32)
+                else:
+                    s = zs2[p, j, z // 2].astype(f32)
+                    for n in range(NZ - 1):
+                        s = s + dzb[n, j - 1].astype(f32)
                 s = jnp.concatenate([s[8 * h : 8 * h + 8] for h in range(DCW // 128)], axis=1)
                 cols = slice(j * DCW, j * DCW + DCW)
-                out[:, cols] = (stream[:, cols] + s).astype(bf16)
+                outs[1, :, cols] = (stream[:, cols] + s).astype(bf16)
 
     combine(6)
-    finish_merge(0)
     combine(7)
+    finish_merge(1)
     for i in I_ORDER:
         spread(0, i)
-    finish_merge(1)
-    for i in I_ORDER:
-        forward(0, i)
+    pass_rest(0)
+    pass_rest(1)
     for i in I_ORDER:
         spread(1, i)
     gathered(0)
     rebuild(0)
     wait_bytes(wgu, w_sem)
     project(0)
-    for i in I_ORDER:
-        forward(1, i)
     sum_cores(0)
     gathered(1)
     rebuild(1)
@@ -423,23 +492,29 @@
     activate(1)
     down(0)
     hid_forward(1)
+    down(1)
+    sum_z(0)
     sum_x(0)
-    down(1)
     sum_x(1)
+    sum_z(1)
     finish(0)
     finish(1)
 
     wait_bytes(sbuf.at[pl.ds(1, 3)], ax_s)
     wait_bytes(zs.at[pl.ds(0, 7)], az_s)
-    wait_bytes(ag.at[pl.ds(0, 7)], gz_s)
-    wait_bytes(ag.at[pl.ds(0, 24)], gx_s)
+    wait_bytes(ag.at[pl.ds(0, 7), pl.ds(0, SPLIT)], gz_s)
+    wait_bytes(ag.at[pl.ds(0, 24), pl.ds(0, SPLIT)], gx_s)
+    wait_bytes(ag.at[pl.ds(0, 3), pl.ds(SPLIT, PIECE - SPLIT)], hx_s)
+    wait_bytes(ag.at[pl.ds(0, 28), pl.ds(SPLIT, PIECE - SPLIT)], hz_s)
     wait_bytes(ssc, sc_s)
     wait_bytes(ssr, ss_s)
     wait_bytes(gs, c_s)
     wait_bytes(yb, y_s)
     wait_bytes(hid.at[0, pl.ds(0, 96)], hy_s)
     wait_bytes(hid.at[0], hc_s)
-    wait_bytes(dxb, dx_s)
+    wait_bytes(dxb.at[:, :, pl.ds(1, DCH - 1)], dx_s)
+    wait_bytes(fzb, fz_s)
+    wait_bytes(fxb, fx_s)
     wait_bytes(dzb, dz_s)
 
 
@@ -447,8 +522,14 @@
     vmem = pl.BlockSpec(memory_space=pltpu.VMEM)
     hbm = pl.BlockSpec(memory_space=pl.ANY)
     dma = pltpu.SemaphoreType.DMA
-    shape = jax.ShapeDtypeStruct((OWN, LOCAL), bf16)
+    shape = pltpu.VMEM((2, OWN, LOCAL), bf16)
     scratch = [
+        pltpu.VMEM((256, LOCAL), bf16),
+        pltpu.VMEM((CTX, HD), bf16),
+        pltpu.VMEM((CTX, HD), bf16),
+        pltpu.VMEM((OWN, LOCAL), bf16),
+        pltpu.VMEM((1, LOCAL), f32),
+        dma, dma, dma, dma, dma,
         pltpu.VMEM((HD + 16, CTX), bf16),
         pltpu.VMEM((CTX, COLS), f32),
         pltpu.VMEM((NX, NZ, PIECE, 128), bf16),
@@ -473,12 +554,17 @@
         pltpu.VMEM((2, DCH, NX, 128, 128), bf16),
         pltpu.VMEM((2, NX - 1, DCH, 128, 128), bf16),
         pltpu.VMEM((2, DCH, 4, 32, 128), bf16),
-        pltpu.VMEM((NZ - 1, DCH, 32, 128), bf16),
+        pltpu.VMEM((NZ - 1, DCH - 1, 32, 128), bf16),
+        pltpu.VMEM((NZ - 1, NX, 32, 128), bf16),
+        pltpu.VMEM((NX, 32, 128), bf16),
+        pltpu.VMEM((NX - 1, 32, 128), bf16),
         dma, dma,
         dma, dma((NX - 1, NZ)),
         dma, dma((NZ - 1,)),
         dma, dma((NZ - 1,)),
-        dma, dma((2, NZ)), dma((2, 2)),
+        dma, dma((NX - 1, NZ)),
+        dma, dma((NX - 1,)),
+        dma, dma((NZ - 1,)),
         dma, dma((2,)),
         dma, dma((2, NY - 1)),
         dma, dma((2, FCH)),
@@ -487,12 +573,14 @@
         dma, dma((2,)),
         dma, dma((2, NX - 1, DCH)),
         dma, dma((NZ - 1,)),
+        dma, dma((NZ - 1,)),
+        dma, dma((NX - 1,)),
     ]
-    return pl.pallas_call(
+    outs = pl.pallas_call(
         kernel,
-        out_shape=(shape, shape),
-        in_specs=[vmem] * 5 + [hbm] * 3,
-        out_specs=(vmem, vmem),
+        out_shape=shape,
+        in_specs=[hbm] * 8,
+        out_specs=vmem,
         scratch_shapes=scratch,
         name="layer",
         compiler_params=pltpu.CompilerParams(
@@ -501,6 +589,7 @@
     )(
         queries, cache_keys, cache_values, residual, norm_gain.reshape(1, LOCAL), w_gate, w_up, w_down
     )
+    return outs[0], outs[1]
 
 
 def solution(mesh):

time: 82.2 us -> 71.7 us (0.87)
  Pallas kernels: 78.5 us -> 70.3 us
  local copies, waits for them, and re-layouts: 2.75 us -> 0.63 us
    pallas_call x1, Pallas kernels: 78.5 us -> 70.3 us  [body(): pl.pallas_call(kernel, out_shape=shape, in_specs=[hbm] * 8, out_specs=vme...]
    unnamed x2 -> x0, local copies, waits for them, and re-layouts: 2.75 us -> none
where the time goes in v3:
time: 71.7 us; the launch traced here: 71.6 us
  Pallas kernels  70.3 us (98%)
    pallas_call x1, Pallas kernels, body(): pl.pallas_call(kernel, out_shape=shape, in_specs=[hbm] * 8, out_specs=vme...  70.3 us

profile of v3, /device:TPU:32, one launch (start us, length us, event | category | flops | bytes accessed | tf_op | source)
XLA Modules:
  0.0 71.6 jit_solution(5237563709878601506)
XLA Ops:
  0.6 70.3 %layer.1 = bf16[2,8,2048]{2,1,0:T(8,128)(2,1)S(1)} custom-call(bf16[256,2048]{1,0:T(8,128)(2,1)} %q_in.1, bf16[2560,128]{1,0:T(8,128)(2,1)} %k_in.1, bf16[2560,128]{1,0:T(8,128)(2,1)} %v_in.1, bf16[8,2048]{1,0:T(8,128)(2,1)} %res_in.1, f32[1,2048]{1,0:T(1,128)} %bitcast.5, bf16[2048,896]{1,0:T(8,128)(2,1)} %wg.1, bf16[2048,896]{1,0:T(8,128)(2,1)} %wu.1, ...), custom_call_target="tpu_custom_call" | custom-call | tf_op jit(solution)/shard_map/layer/pallas_call | solution.py:579
  71.0 0.6 slice_bitcast_fusion

commit v4 on v3

--- a/solution.py
+++ b/solution.py
@@ -58,7 +58,7 @@
 def kernel(
     q_in, k_in, v_in, res_in, gain_in, wg, wu, wd, outs,
     q, k, v, res, gain, q_sem, k_sem, v_sem, res_sem, gain_sem,
-    vt, sc, sbuf, xbuf, zs, zbuf, stream, ag, xn, ssb, ssc, ssr, wgu, wdv,
+    vt, sc, sbuf, xbuf, zs, zbuf, stream, ag, ginv, xn, ssb, ssc, ssr, wgu, wdv,
     gacc, gs, cbuf, ys, yb, hid, dsf, ds, dxb, zs2, dzb, fzb, fzs, fxb,
     w_sem, d_sem, ax_s, ax_r, az_s, az_r, gz_s, gz_r, gx_s, gx_r, hx_s, hx_r, hz_s, hz_r,
     sc_s, sc_r, ss_s, ss_r, c_s, c_r, y_s, y_r, hy_s, hy_r, hc_s, hc_r, dx_s, dx_r, dz_s, dz_r, fz_s, fz_r, fx_s, fx_r,
@@ -198,7 +198,7 @@
         return ag.at[src, pl.ds(0, SPLIT)]
 
     def rest(src):
-        return ag.at[src, pl.ds(SPLIT, PIECE - SPLIT)]
+        return ag.at[src, pl.ds(SPLIT, 128 - SPLIT)]
 
     def rest_x(src, dx):
         return remote(rest(src), rest(src), hx_s, hx_r.at[dx - 1], at_x(dx))
@@ -229,11 +229,9 @@
             outs[0] = att
             st = res[...].astype(f32) + att.astype(f32)
             stream[...] = st
-            squares = jnp.broadcast_to(jnp.sum(st * st, axis=1, keepdims=True), (OWN, 128))
             t = st * gain[...]
             rows = jnp.concatenate([t[:, 128 * h : 128 * h + 128] for h in range(16)], axis=0)
-            ag[kv, :128, :] = rows.astype(bf16)
-            ag[kv, 128:PIECE, :] = jnp.concatenate(split2(squares), axis=0).astype(bf16)
+            ag[kv] = rows.astype(bf16)
             for o in FAR:
                 gather_z(o).start()
             for dx in (2, 1, 3):
@@ -242,13 +240,9 @@
     def attend(j, top):
         top = step(j, top)
 
-        @pl.when(j >= 2)
+        @pl.when(j >= 3)
         def _():
-            combine(j - 2)
-
-        @pl.when(j == NZ - 1)
-        def _():
-            finish_merge(0)
+            combine(j - 3)
 
         return top
 
@@ -280,7 +274,11 @@
 
             @pl.when(o != 0)
             def _():
-                wait_bytes(ag.at[pl.ds(0, NX), pl.ds(SPLIT, PIECE - SPLIT)], hz_r.at[o - 1])
+                wait_bytes(ag.at[pl.ds(0, NX), pl.ds(SPLIT, 128 - SPLIT)], hz_r.at[o - 1])
+
+    def row_squares(rows):
+        st = rows * ginv[...]
+        return jnp.sum((st * st).reshape(16, OWN, 128), axis=0)
 
     def rebuild(p):
         def pair(i, _):
@@ -291,7 +289,7 @@
             for h in range(16):
                 tile = jnp.concatenate([a[8 * h : 8 * h + 8], b[8 * h : 8 * h + 8]], axis=0)
                 xn[p, rows, 128 * h : 128 * h + 128] = tile.astype(bf16)
-            ssb[p, rows, :] = jnp.concatenate([a[128:136] + a[136:144], b[128:136] + b[136:144]], axis=0)
+            ssb[p, rows, :] = jnp.concatenate([row_squares(a), row_squares(b)], axis=0)
             return 0
 
         lax.fori_loop(0, 8, pair, 0)
@@ -358,7 +356,7 @@
         squares = ssb[p, own16, :]
         for n in range(NY - 1):
             squares = squares + ssr[p, n]
-        scale = lax.rsqrt(squares / D + EPSILON)
+        scale = lax.rsqrt(jnp.sum(squares, axis=1, keepdims=True) / D + EPSILON)
         for dy in range(1, NY):
             wait_bytes(yb.at[p, dy - 1], y_r.at[p, dy - 1])
         for j in range(FCH):
@@ -468,6 +466,8 @@
                 cols = slice(j * DCW, j * DCW + DCW)
                 outs[1, :, cols] = (stream[:, cols] + s).astype(bf16)
 
+    finish_merge(0)
+    combine(5)
     combine(6)
     combine(7)
     finish_merge(1)
@@ -477,6 +477,8 @@
     pass_rest(1)
     for i in I_ORDER:
         spread(1, i)
+    inverse = jnp.broadcast_to(1.0 / gain[...], (OWN, LOCAL))
+    ginv[...] = jnp.concatenate([inverse[:, 128 * h : 128 * h + 128] for h in range(16)], axis=0)
     gathered(0)
     rebuild(0)
     wait_bytes(wgu, w_sem)
@@ -504,8 +506,8 @@
     wait_bytes(zs.at[pl.ds(0, 7)], az_s)
     wait_bytes(ag.at[pl.ds(0, 7), pl.ds(0, SPLIT)], gz_s)
     wait_bytes(ag.at[pl.ds(0, 24), pl.ds(0, SPLIT)], gx_s)
-    wait_bytes(ag.at[pl.ds(0, 3), pl.ds(SPLIT, PIECE - SPLIT)], hx_s)
-    wait_bytes(ag.at[pl.ds(0, 28), pl.ds(SPLIT, PIECE - SPLIT)], hz_s)
+    wait_bytes(ag.at[pl.ds(0, 3), pl.ds(SPLIT, 128 - SPLIT)], hx_s)
+    wait_bytes(ag.at[pl.ds(0, 28), pl.ds(SPLIT, 128 - SPLIT)], hz_s)
     wait_bytes(ssc, sc_s)
     wait_bytes(ssr, ss_s)
     wait_bytes(gs, c_s)
@@ -537,7 +539,8 @@
         pltpu.VMEM((NZ, PIECE, 128), bf16),
         pltpu.VMEM((NZ - 1, PIECE, 128), bf16),
         pltpu.VMEM((OWN, LOCAL), f32),
-        pltpu.VMEM((NKV, PIECE, 128), bf16),
+        pltpu.VMEM((NKV, 128, 128), bf16),
+        pltpu.VMEM((128, 128), f32),
         pltpu.VMEM((2, 128, LOCAL), bf16),
         pltpu.VMEM((2, 128, 128), f32),
         pltpu.VMEM((2, 64, 128), f32),

time: 71.7 us -> 70.1 us (0.978)
  Pallas kernels: 70.3 us -> 68.7 us
    pallas_call x1, Pallas kernels: 70.3 us -> 68.7 us  [body(): pl.pallas_call(kernel, out_shape=shape, in_specs=[hbm] * 8, out_specs=vme...]
where the time goes in v4:
time: 70.1 us; the launch traced here: 70 us
  Pallas kernels  68.7 us (98%)
    pallas_call x1, Pallas kernels, body(): pl.pallas_call(kernel, out_shape=shape, in_specs=[hbm] * 8, out_specs=vme...  68.7 us

profile of v4, /device:TPU:32, one launch (start us, length us, event | category | flops | bytes accessed | tf_op | source)
XLA Modules:
  0.0 70.0 jit_solution(738712651956569638)
XLA Ops:
  0.6 68.7 %layer.1 = bf16[2,8,2048]{2,1,0:T(8,128)(2,1)S(1)} custom-call(bf16[256,2048]{1,0:T(8,128)(2,1)} %q_in.1, bf16[2560,128]{1,0:T(8,128)(2,1)} %k_in.1, bf16[2560,128]{1,0:T(8,128)(2,1)} %v_in.1, bf16[8,2048]{1,0:T(8,128)(2,1)} %res_in.1, f32[1,2048]{1,0:T(1,128)} %bitcast.5, bf16[2048,896]{1,0:T(8,128)(2,1)} %wg.1, bf16[2048,896]{1,0:T(8,128)(2,1)} %wu.1, ...), custom_call_target="tpu_custom_call" | custom-call | tf_op jit(solution)/shard_map/layer/pallas_call | solution.py:582
  69.4 0.6 slice_bitcast_fusion

commit v5 on v4

--- a/solution.py
+++ b/solution.py
@@ -475,10 +475,10 @@
         spread(0, i)
     pass_rest(0)
     pass_rest(1)
+    inverse = jnp.broadcast_to(1.0 / gain[...], (OWN, LOCAL))
+    ginv[...] = jnp.concatenate([inverse[:, 128 * h : 128 * h + 128] for h in range(16)], axis=0)
     for i in I_ORDER:
         spread(1, i)
-    inverse = jnp.broadcast_to(1.0 / gain[...], (OWN, LOCAL))
-    ginv[...] = jnp.concatenate([inverse[:, 128 * h : 128 * h + 128] for h in range(16)], axis=0)
     gathered(0)
     rebuild(0)
     wait_bytes(wgu, w_sem)

time: 70.1 us -> 70.1 us (level)
  no operation moved by 1% of the time
where the time goes in v5:
time: 70.1 us; the launch traced here: 70 us
  Pallas kernels  68.7 us (98%)
    pallas_call x1, Pallas kernels, body(): pl.pallas_call(kernel, out_shape=shape, in_specs=[hbm] * 8, out_specs=vme...  68.7 us

profile of v5, /device:TPU:32, one launch (start us, length us, event | category | flops | bytes accessed | tf_op | source)
XLA Modules:
  0.0 70.0 jit_solution(4005877686850204977)
XLA Ops:
  0.6 68.7 %layer.1 = bf16[2,8,2048]{2,1,0:T(8,128)(2,1)S(1)} custom-call(bf16[256,2048]{1,0:T(8,128)(2,1)} %q_in.1, bf16[2560,128]{1,0:T(8,128)(2,1)} %k_in.1, bf16[2560,128]{1,0:T(8,128)(2,1)} %v_in.1, bf16[8,2048]{1,0:T(8,128)(2,1)} %res_in.1, f32[1,2048]{1,0:T(1,128)} %bitcast.5, bf16[2048,896]{1,0:T(8,128)(2,1)} %wg.1, bf16[2048,896]{1,0:T(8,128)(2,1)} %wu.1, ...), custom_call_target="tpu_custom_call" | custom-call | tf_op jit(solution)/shard_map/layer/pallas_call | solution.py:582
  69.3 0.6 slice_bitcast_fusion
